TPU v7x, 32 devices: a whole 2x2x4 slice. The times are simulated.
32 devices in a mesh: tm: 16 (over z, y, core), mp: 2 (over x).
Axes of the slice: x: 2, y: 2, z: 4, core: 2. Of those that a mesh axis runs over, the one named last changes fastest.
Arguments:
- queries: bfloat16 [4096, 1024], P('tm', 'mp'), may hold values from -8 to 8
- score_tokens: bfloat16 [2048, 1024], P('tm'), may hold values from -8 to 8
- key_weight: bfloat16 [1024, 256], P(None, 'mp'), may hold values from -0.1875 to 0.1875
- value_weight: bfloat16 [1024, 256], P(None, 'mp'), may hold values from -0.1875 to 0.1875
- d_attended: bfloat16 [4096, 1024], P('tm', 'mp'), may hold values from -6 to 6
- band_lo: int32 [16], P('tm'), may hold values from 0 to 13, as said below
- band_hi: int32 [16], P('tm'), may hold values from 1 to 16, as said below
- lead_offset: int32 [16], P('tm'), may hold values from 0 to 127
Outputs:
- attended: bfloat16 [4096, 1024], P('tm', 'mp')
- d_queries: bfloat16 [4096, 1024], P('tm', 'mp')
- d_score_tokens: bfloat16 [2048, 1024], P('tm', 'mp')
- d_key_weight: float32 [1024, 256], P('tm', 'mp')
- d_value_weight: float32 [1024, 256], P('tm', 'mp')
Inputs may be any that keep to these rules, and one draw needn't show every extreme that they name: band_lo never falls from one frame block to the next, and t - 2 <= band_lo[t] <= t for frame block t. band_lo[t] < band_hi[t] <= band_lo[t] + 3; some t has band_lo[t] = t and band_hi[t] = t + 3.
All inputs are finite; a program needn't handle non-finite values.
Results may differ from a plain program's by a relative error of at most 0.013.
Values may be sent and summed in bfloat16 or wider, within the bound.
A program may use at most 64 MiB of HBM per device.

v0:
```python
import jax
import jax.numpy as jnp
from jax import lax
from jax.sharding import PartitionSpec as P

HQ = 16
KVH = 4
HD = 64
MAXW = 3


softcap = 5.0


def from_behind(value, axis, steps):
    count = lax.axis_size(axis)
    first, last = (max(0, -steps), min(count, count - steps))
    return lax.ppermute(value, axis, [(source, source + steps) for source in range(first, last)])


def shards(
    queries, score_tokens, key_weight, value_weight, d_attended, band_lo, band_hi, lead_offset
):
    frames = queries.shape[0]
    blocklen = score_tokens.shape[0]
    groups = key_weight.shape[1] // HD
    head_ratio = HQ // KVH
    scaling = HD ** (-0.5)
    position = lax.axis_index("tm")
    band_first = band_lo[0]
    band_last = band_hi[0]
    margin_value = lead_offset[0]
    key_rows = jnp.dot(score_tokens, key_weight, preferred_element_type=jnp.float32).astype(
        jnp.bfloat16
    )
    value_rows = jnp.dot(score_tokens, value_weight, preferred_element_type=jnp.float32).astype(
        jnp.bfloat16
    )
    packed = jnp.stack([key_rows, value_rows])
    arrived = {0: packed}
    behind_block = packed
    front_block = packed
    for hop_count in range(1, MAXW):
        behind_block = from_behind(behind_block, "tm", 1)
        front_block = from_behind(front_block, "tm", -1)
        arrived[-hop_count] = behind_block
        arrived[hop_count] = front_block
    table = jnp.stack([arrived[offset] for offset in range(1 - MAXW, MAXW)])
    q_heads = queries.reshape(frames, groups, head_ratio, HD)
    grads_out = d_attended.reshape(frames, groups, head_ratio, HD)
    tile_shape = (groups, head_ratio, frames, blocklen)

    def slot_place(slot_index):
        return band_first + slot_index - position + MAXW - 1

    def slot_rows(slot_index):
        chosen = lax.dynamic_index_in_dim(table, slot_place(slot_index), 0, keepdims=False)
        return (chosen[0].reshape(blocklen, groups, HD), chosen[1].reshape(blocklen, groups, HD))

    def tile_logits(key_tile, slot_index):
        raw = (
            jnp.einsum("fgrd,sgd->grfs", q_heads, key_tile, preferred_element_type=jnp.float32)
            * scaling
        )
        capped = jnp.tanh(raw / softcap)
        column = (band_first + slot_index) * blocklen + jnp.arange(blocklen, dtype=jnp.int32)
        allowed = column >= band_first * blocklen + margin_value
        expo = jnp.where(allowed, jnp.exp(softcap * capped), jnp.float32(0.0))
        return (capped, expo)

    live_flags = [band_first + slot_index < band_last for slot_index in range(MAXW)]
    slot_tiles = [slot_rows(slot_index) for slot_index in range(MAXW)]
    expo_tiles = []
    row_total = jnp.zeros(tile_shape[:3], jnp.float32)
    for slot_index in range(MAXW):
        key_tile = slot_tiles[slot_index][0]
        expo = lax.cond(
            live_flags[slot_index],
            lambda: tile_logits(key_tile, slot_index)[1],
            lambda: jnp.zeros(tile_shape, jnp.float32),
        )
        expo_tiles.append(expo)
        row_total = row_total + jnp.sum(expo, -1)
    mixed = jnp.zeros((frames, groups, head_ratio, HD), jnp.float32)
    for slot_index in range(MAXW):
        value_tile = slot_tiles[slot_index][1]
        expo = expo_tiles[slot_index]
        mixed = mixed + lax.cond(
            live_flags[slot_index],
            lambda: jnp.einsum(
                "grfs,sgd->fgrd",
                (expo / row_total[..., None]).astype(jnp.bfloat16),
                value_tile,
                preferred_element_type=jnp.float32,
            ),
            lambda: jnp.zeros((frames, groups, head_ratio, HD), jnp.float32),
        )
    attended = mixed.astype(jnp.bfloat16).reshape(frames, -1)
    delta = jnp.sum(grads_out.astype(jnp.float32) * mixed, -1).transpose(1, 2, 0)
    query_acc = jnp.zeros((frames, groups, head_ratio, HD), jnp.float32)
    back_table = jnp.zeros((2 * MAXW - 1, 2, blocklen, groups * HD), jnp.float32)
    for slot_index in range(MAXW):
        key_tile, value_tile = slot_tiles[slot_index]

        def backward_tile():
            capped, expo = tile_logits(key_tile, slot_index)
            probs = expo / row_total[..., None]
            probs_low = probs.astype(jnp.bfloat16)
            d_probs = jnp.einsum(
                "fgrd,sgd->grfs", grads_out, value_tile, preferred_element_type=jnp.float32
            )
            d_raw = (probs * (d_probs - delta[..., None]) * (1.0 - capped * capped)).astype(
                jnp.bfloat16
            )
            query_part = jnp.einsum(
                "grfs,sgd->fgrd", d_raw, key_tile, preferred_element_type=jnp.float32
            )
            key_part = (
                jnp.einsum("grfs,fgrd->sgd", d_raw, q_heads, preferred_element_type=jnp.float32)
                * scaling
            )
            value_part = jnp.einsum(
                "grfs,fgrd->sgd", probs_low, grads_out, preferred_element_type=jnp.float32
            )
            return (
                query_part,
                jnp.stack([key_part.reshape(blocklen, -1), value_part.reshape(blocklen, -1)]),
            )

        def empty_tile():
            return (
                jnp.zeros((frames, groups, head_ratio, HD), jnp.float32),
                jnp.zeros((2, blocklen, groups * HD), jnp.float32),
            )

        query_part, pair_part = lax.cond(live_flags[slot_index], backward_tile, empty_tile)
        query_acc = query_acc + query_part
        back_table = lax.dynamic_update_index_in_dim(
            back_table, pair_part, slot_place(slot_index), 0
        )
    d_queries = (query_acc * scaling).astype(jnp.bfloat16).reshape(frames, -1)
    gathered = back_table[MAXW - 1]
    for offset in range(1 - MAXW, MAXW):
        if offset != 0:
            gathered = gathered + from_behind(
                back_table[offset + MAXW - 1].astype(jnp.bfloat16), "tm", offset
            ).astype(jnp.float32)
    key_grad = gathered[0].astype(jnp.bfloat16)
    value_grad = gathered[1].astype(jnp.bfloat16)
    contract = (((1,), (1,)), ((), ()))
    score_term = lax.dot_general(
        key_grad, key_weight, contract, preferred_element_type=jnp.float32
    ) + lax.dot_general(value_grad, value_weight, contract, preferred_element_type=jnp.float32)
    d_score_tokens = lax.psum_scatter(
        score_term.astype(jnp.bfloat16), "mp", scatter_dimension=1, tiled=True
    )
    both_grads = jnp.concatenate([key_grad, value_grad], 1)
    over_rows = (((0,), (0,)), ((), ()))
    own_rows = score_tokens.shape[1] // lax.axis_size("tm")
    total_grad = lax.psum(
        lax.dot_general(score_tokens, both_grads, over_rows, preferred_element_type=jnp.float32),
        "tm",
    )
    own_grad = lax.dynamic_slice_in_dim(total_grad, position * own_rows, own_rows, 0)
    half_width = key_grad.shape[1]
    return (attended, d_queries, d_score_tokens, own_grad[:, :half_width], own_grad[:, half_width:])


def solution(mesh):
    in_specs = (
        P("tm", "mp"),
        P("tm", None),
        P(None, "mp"),
        P(None, "mp"),
        P("tm", "mp"),
        P("tm"),
        P("tm"),
        P("tm"),
    )
    out_specs = (P("tm", "mp"), P("tm", "mp"), P("tm", "mp"), P("tm", "mp"), P("tm", "mp"))
    return jax.shard_map(shards, mesh=mesh, in_specs=in_specs, out_specs=out_specs, check_vma=False)
```

profile of v0, /device:TPU:0, one launch (start us, length us, event | category | flops | bytes accessed | tf_op | source)
XLA Modules:
  0.0 188.0 jit_solution(16716619187905210609)
XLA Ops:
  10.5 2.4 %collective-permute-start = (bf16[2,128,128]{1,2,0:T(8,128)(2,1)S(1)}, bf16[2,128,128]{1,2,0:T(8,128)(2,1)S(1)}, u32[]{:S(2)}, u32[]{:S(2)}) collective-permute-start(bf16[2,128,128]{1,2,0:T(8,128)(2,1)S(1)} %pad_maximum_fusion), channel_id=1, source_target_pairs={{0,2},{2,4},{4,6},{6,8},{8,10},{10,12},{12,14},{14,16},{16,18},{18... | collective-permute-start | bytes 196616 | tf_op jit(solution)/shard_map/ppermute | solution.py:18
  14.2 5.2 %collective-permute-start.1 = (bf16[2,128,128]{1,2,0:T(8,128)(2,1)S(1)}, bf16[2,128,128]{1,2,0:T(8,128)(2,1)S(1)}, u32[]{:S(2)}, u32[]{:S(2)}) collective-permute-start(bf16[2,128,128]{1,2,0:T(8,128)(2,1)S(1)} %collective-permute-done), channel_id=1, source_target_pairs={{0,2},{2,4},{4,6},{6,8},{8,10},{10,12},{12,14},{14,16},{16,18},{18... | collective-permute-start | bytes 196616 | tf_op jit(solution)/shard_map/ppermute | solution.py:18
  23.2 3.0 %collective-permute-done.3 = bf16[2,128,128]{1,2,0:T(8,128)(2,1)S(1)} collective-permute-done((bf16[2,128,128]{1,2,0:T(8,128)(2,1)S(1)}, bf16[2,128,128]{1,2,0:T(8,128)(2,1)S(1)}, u32[]{:S(2)}, u32[]{:S(2)}) %collective-permute-start.3) | collective-permute-done | bytes 65568 | tf_op jit(solution)/shard_map/ppermute | solution.py:18
  26.9 2.5 %conditional.10 = (f32[2,4,256,128]{2,3,1,0:T(8,128)S(1)}, f32[2,4,256]{2,1,0:T(4,128)S(1)}) conditional(s32[]{:T(128)} %convert_element_type.99, () %tuple.89, (s32[]{:T(128)}, s32[]{:T(128)}, bf16[128,2,64]{0,2,1:T(8,128)(2,1)S(1)}, bf16[256,2,4,64]{0,3,2,1:T(8,128)(2,1)S(1)}) %tuple.161), branch_computations={%region_3.4_spmd, %region_4.6_spmd} | conditional | flops 34601220 | bytes 1352008 | solution.py:77
  29.3 2.5 %conditional.11 = (f32[2,4,256,128]{2,3,1,0:T(8,128)S(1)}, f32[2,4,256]{2,1,0:T(4,128)S(1)}) conditional(s32[]{:T(128)} %convert_element_type.100, () %tuple.91, (s32[]{:T(128)}, s32[]{:T(128)}, bf16[128,2,64]{0,2,1:T(8,128)(2,1)S(1)}, bf16[256,2,4,64]{0,3,2,1:T(8,128)(2,1)S(1)}) %tuple.159), branch_computations={%region_6.7_spmd, %region_7.9_spmd} | conditional | flops 34601220 | bytes 1352008 | solution.py:77
  31.9 1.8 conditional.9
  34.7 3.1 %conditional.13 = (f32[256,2,4,64]{0,3,2,1:T(8,128)S(1)}) conditional(s32[]{:T(128)} %convert_element_type.99, () %tuple.94, (f32[2,4,256]{2,1,0:T(4,128)S(1)}, f32[2,4,256,128]{2,3,1,0:T(8,128)S(1)}, bf16[128,2,64]{0,2,1:T(8,128)(2,1)S(1)}) %tuple.174), branch_computations={%region_11.12_spmd, %region_12.13_spmd} | conditional | flops 34078720 | bytes 3710984 | solution.py:88
  34.7 1.3 copy.42
  36.0 1.7 convolution_bitcast_fusion.1
  37.8 4.3 %conditional.12 = (f32[256,2,4,64]{0,3,2,1:T(8,128)S(1)}) conditional(s32[]{:T(128)} %convert_element_type.96, () %tuple.86, (f32[2,4,256]{2,1,0:T(4,128)S(1)}, f32[2,4,256,128]{2,3,1,0:T(8,128)}, bf16[128,2,64]{0,2,1:T(8,128)(2,1)S(1)}) %tuple.175), branch_computations={%region_9.10_spmd, %region_10.11_spmd} | conditional | flops 34078720 | bytes 3710984 | solution.py:88
  37.8 2.5 %copy.41 = f32[2,4,256,128]{3,2,1,0:T(8,128)} copy(f32[2,4,256,128]{2,3,1,0:T(8,128)} %get-tuple-element.197) | data formatting | bytes 2097152 | tf_op jit(solution)/shard_map
  40.3 1.7 convolution_bitcast_fusion
  42.1 3.1 %conditional.14 = (f32[256,2,4,64]{0,3,2,1:T(8,128)S(1)}) conditional(s32[]{:T(128)} %convert_element_type.100, () %tuple.96, (f32[2,4,256]{2,1,0:T(4,128)S(1)}, f32[2,4,256,128]{2,3,1,0:T(8,128)S(1)}, bf16[128,2,64]{0,2,1:T(8,128)(2,1)S(1)}) %tuple.176), branch_computations={%region_13.14_spmd, %region_14.15_spmd} | conditional | flops 34078720 | bytes 3710984 | solution.py:88
  42.1 1.3 copy.43
  43.5 1.7 convolution_bitcast_fusion.2
  45.2 1.8 multiply_reduce_fusion
  47.0 4.5 %conditional.15 = (f32[256,2,4,64]{0,3,2,1:T(8,128)S(1)}, f32[1,2,128,128]{2,3,1,0:T(8,128)S(1)}) conditional(s32[]{:T(128)} %convert_element_type.96, () %tuple.98, (s32[]{:T(128)}, s32[]{:T(128)}, bf16[128,2,64]{0,2,1:T(8,128)(2,1)S(1)}, bf16[256,2,4,64]{0,3,2,1:T(8,128)(2,1)S(1)}, f32[2,4,256]{2,1,0:T(4,128)S(1)}, ...), branch_computations={%region_16.17_spmd, %region_17.18_spmd} | conditional | flops 171491584 | bytes 8380988 | solution.py:136
  52.5 3.8 %conditional.16 = (f32[256,2,4,64]{0,3,2,1:T(8,128)S(1)}, f32[1,2,128,128]{2,3,1,0:T(8,128)S(1)}) conditional(s32[]{:T(128)} %convert_element_type.99, () %tuple.100, (s32[]{:T(128)}, s32[]{:T(128)}, bf16[128,2,64]{0,2,1:T(8,128)(2,1)S(1)}, bf16[256,2,4,64]{0,3,2,1:T(8,128)(2,1)S(1)}, f32[2,4,256]{2,1,0:T(4,128)S(1)}, ...), branch_computations={%region_18.19_spmd, %region_19.20_spmd} | conditional | flops 171491584 | bytes 6808008 | solution.py:136
  56.3 7.6 %conditional.17 = (f32[256,2,4,64]{0,3,2,1:T(8,128)S(1)}, f32[1,2,128,128]{2,3,1,0:T(8,128)S(1)}) conditional(s32[]{:T(128)} %convert_element_type.100, () %tuple.102, (s32[]{:T(128)}, s32[]{:T(128)}, bf16[128,2,64]{0,2,1:T(8,128)(2,1)}, bf16[256,2,4,64]{0,3,2,1:T(8,128)(2,1)S(1)}, f32[2,4,256]{2,1,0:T(4,128)S(1)}, ...), branch_computations={%region_20.21_spmd, %region_21.22_spmd} | conditional | flops 171491584 | bytes 9036316 | solution.py:136
  60.1 1.5 fusion.53
  66.6 5.5 %collective-permute-start.6 = (bf16[2,128,128]{1,2,0:T(8,128)(2,1)S(1)}, bf16[2,128,128]{1,2,0:T(8,128)(2,1)S(1)}, u32[]{:S(2)}, u32[]{:S(2)}) collective-permute-start(bf16[2,128,128]{1,2,0:T(8,128)(2,1)S(1)} %get-tuple-element.222), channel_id=1, source_target_pairs={{0,2},{2,4},{4,6},{6,8},{8,10},{10,12},{12,14},{14,16},{16,18},{18... | collective-permute-start | bytes 196616 | tf_op jit(solution)/shard_map/ppermute | solution.py:18
  72.1 4.3 %collective-permute-start.7 = (bf16[2,128,128]{1,2,0:T(8,128)(2,1)S(1)}, bf16[2,128,128]{1,2,0:T(8,128)(2,1)S(1)}, u32[]{:S(2)}, u32[]{:S(2)}) collective-permute-start(bf16[2,128,128]{1,2,0:T(8,128)(2,1)S(1)} %get-tuple-element.221), channel_id=1, source_target_pairs={{0,4},{2,6},{4,8},{6,10},{8,12},{10,14},{12,16},{14,18},{16,20},{1... | collective-permute-start | bytes 196616 | tf_op jit(solution)/shard_map/ppermute | solution.py:18
  76.4 1.9 collective-permute-done.7
  83.7 94.5 %all-reduce.2.cloned.1.call-done = f32[1024,256]{0,1:T(8,128)} async-done(((f32[1024,256]{0,1:T(8,128)}), f32[1024,256]{0,1:T(8,128)}) %all-reduce.2.cloned.1.call-update) | async-done | bytes 1048592 | tf_op jit(solution)/shard_map/psum | solution.py:160
  (118 shorter events, 29.7 us)
Async XLA Ops:
  8.0 1.0 copy-start
  8.0 2.2 %copy-start.3 = (bf16[1024,128]{1,0:T(8,128)(2,1)S(1)}, bf16[1024,128]{1,0:T(8,128)(2,1)}, u32[]{:S(2)}) copy-start(bf16[1024,128]{1,0:T(8,128)(2,1)} %param.29) | copy-start | bytes 786436
  8.0 170.1 %all-reduce.2.cloned.1.call-start = ((), (), s32[]{:S(2)}) async-start(), calls=%async_computation.2 | async-start | bytes 2097152 | tf_op jit(solution)/shard_map/psum | solution.py:160
  10.2 9.8 %copy-start.17 = (bf16[256,512]{1,0:T(8,128)(2,1)S(1)}, bf16[256,512]{1,0:T(8,128)(2,1)}, u32[]{:S(2)}) copy-start(bf16[256,512]{1,0:T(8,128)(2,1)} %param.26) | copy-start | bytes 786436
  10.5 3.7 %collective-permute-start = (bf16[2,128,128]{1,2,0:T(8,128)(2,1)S(1)}, bf16[2,128,128]{1,2,0:T(8,128)(2,1)S(1)}, u32[]{:S(2)}, u32[]{:S(2)}) collective-permute-start(bf16[2,128,128]{1,2,0:T(8,128)(2,1)S(1)} %pad_maximum_fusion), channel_id=1, source_target_pairs={{0,2},{2,4},{4,6},{6,8},{8,10},{10,12},{12,14},{14,16},{16,18},{18... | collective-permute-start | bytes 196616 | tf_op jit(solution)/shard_map/ppermute | solution.py:18
  12.9 9.0 %collective-permute-start.2 = (bf16[2,128,128]{1,2,0:T(8,128)(2,1)S(1)}, bf16[2,128,128]{1,2,0:T(8,128)(2,1)S(1)}, u32[]{:S(2)}, u32[]{:S(2)}) collective-permute-start(bf16[2,128,128]{1,2,0:T(8,128)(2,1)S(1)} %pad_maximum_fusion), channel_id=1, source_target_pairs={{2,0},{4,2},{6,4},{8,6},{10,8},{12,10},{14,12},{16,14},{18,16},{20... | collective-permute-start | bytes 196616 | tf_op jit(solution)/shard_map/ppermute | solution.py:18
  14.2 8.9 %collective-permute-start.1 = (bf16[2,128,128]{1,2,0:T(8,128)(2,1)S(1)}, bf16[2,128,128]{1,2,0:T(8,128)(2,1)S(1)}, u32[]{:S(2)}, u32[]{:S(2)}) collective-permute-start(bf16[2,128,128]{1,2,0:T(8,128)(2,1)S(1)} %collective-permute-done), channel_id=1, source_target_pairs={{0,2},{2,4},{4,6},{6,8},{8,10},{10,12},{12,14},{14,16},{16,18},{18... | collective-permute-start | bytes 196616 | tf_op jit(solution)/shard_map/ppermute | solution.py:18
  20.0 1.0 copy-start.18
  21.8 4.4 %collective-permute-start.3 = (bf16[2,128,128]{1,2,0:T(8,128)(2,1)S(1)}, bf16[2,128,128]{1,2,0:T(8,128)(2,1)S(1)}, u32[]{:S(2)}, u32[]{:S(2)}) collective-permute-start(bf16[2,128,128]{1,2,0:T(8,128)(2,1)S(1)} %collective-permute-done.2), channel_id=1, source_target_pairs={{2,0},{4,2},{6,4},{8,6},{10,8},{12,10},{14,12},{16,14},{18,16},{20... | collective-permute-start | bytes 196616 | tf_op jit(solution)/shard_map/ppermute | solution.py:18
  26.3 3.1 %copy-start.9 = (bf16[1,1,128,128]{2,3,1,0:T(8,128)(2,1)}, bf16[1,1,128,128]{2,3,1,0:T(8,128)(2,1)S(1)}, u32[]{:S(2)}) copy-start(bf16[1,1,128,128]{2,3,1,0:T(8,128)(2,1)S(1)} %get-tuple-element.225) | copy-start | bytes 98308
  26.3 5.6 %copy-start.13 = (bf16[1,1,128,128]{2,3,1,0:T(8,128)(2,1)}, bf16[1,1,128,128]{2,3,1,0:T(8,128)(2,1)S(1)}, u32[]{:S(2)}) copy-start(bf16[1,1,128,128]{2,3,1,0:T(8,128)(2,1)S(1)} %get-tuple-element.227) | copy-start | bytes 98308
  26.3 7.5 %copy-start.20 = (bf16[1,1,128,128]{2,3,1,0:T(8,128)(2,1)}, bf16[1,1,128,128]{2,3,1,0:T(8,128)(2,1)S(1)}, u32[]{:S(2)}) copy-start(bf16[1,1,128,128]{2,3,1,0:T(8,128)(2,1)S(1)} %get-tuple-element.224) | copy-start | bytes 98308
  26.3 15.8 %copy-start.19 = (bf16[1,1,128,128]{2,3,1,0:T(8,128)(2,1)}, bf16[1,1,128,128]{2,3,1,0:T(8,128)(2,1)S(1)}, u32[]{:S(2)}) copy-start(bf16[1,1,128,128]{2,3,1,0:T(8,128)(2,1)S(1)} %get-tuple-element.228) | copy-start | bytes 98308
  33.7 1.0 copy-start.1
  45.2 1.8 copy-start.14
  47.0 1.0 copy-start.15
  47.6 1.7 copy-start.5
  47.6 1.7 copy-start.23
  51.5 1.0 copy-start.4
  64.0 12.4 %collective-permute-start.4 = (bf16[2,128,128]{1,2,0:T(8,128)(2,1)S(1)}, bf16[2,128,128]{1,2,0:T(8,128)(2,1)S(1)}, u32[]{:S(2)}, u32[]{:S(2)}) collective-permute-start(bf16[2,128,128]{1,2,0:T(8,128)(2,1)S(1)} %get-tuple-element.220), channel_id=1, source_target_pairs={{4,0},{6,2},{8,4},{10,6},{12,8},{14,10},{16,12},{18,14},{20,16},{2... | collective-permute-start | bytes 196616 | tf_op jit(solution)/shard_map/ppermute | solution.py:18
  65.3 11.1 %collective-permute-start.5 = (bf16[2,128,128]{1,2,0:T(8,128)(2,1)S(1)}, bf16[2,128,128]{1,2,0:T(8,128)(2,1)S(1)}, u32[]{:S(2)}, u32[]{:S(2)}) collective-permute-start(bf16[2,128,128]{1,2,0:T(8,128)(2,1)S(1)} %get-tuple-element.223), channel_id=1, source_target_pairs={{2,0},{4,2},{6,4},{8,6},{10,8},{12,10},{14,12},{16,14},{18,16},{20... | collective-permute-start | bytes 196616 | tf_op jit(solution)/shard_map/ppermute | solution.py:18
  66.6 9.8 %collective-permute-start.6 = (bf16[2,128,128]{1,2,0:T(8,128)(2,1)S(1)}, bf16[2,128,128]{1,2,0:T(8,128)(2,1)S(1)}, u32[]{:S(2)}, u32[]{:S(2)}) collective-permute-start(bf16[2,128,128]{1,2,0:T(8,128)(2,1)S(1)} %get-tuple-element.222), channel_id=1, source_target_pairs={{0,2},{2,4},{4,6},{6,8},{8,10},{10,12},{12,14},{14,16},{16,18},{18... | collective-permute-start | bytes 196616 | tf_op jit(solution)/shard_map/ppermute | solution.py:18
  72.1 6.2 %collective-permute-start.7 = (bf16[2,128,128]{1,2,0:T(8,128)(2,1)S(1)}, bf16[2,128,128]{1,2,0:T(8,128)(2,1)S(1)}, u32[]{:S(2)}, u32[]{:S(2)}) collective-permute-start(bf16[2,128,128]{1,2,0:T(8,128)(2,1)S(1)} %get-tuple-element.221), channel_id=1, source_target_pairs={{0,4},{2,6},{4,8},{6,10},{8,12},{10,14},{12,16},{14,18},{16,20},{1... | collective-permute-start | bytes 196616 | tf_op jit(solution)/shard_map/ppermute | solution.py:18
  79.6 100.9 %reduce-scatter.2.cloned.1.call-start = ((), (), s32[]{:S(2)}) async-start(), calls=%async_computation.1 | async-start | bytes 393216 | tf_op jit(solution)/shard_map/reduce_scatter | solution.py:154
  (10 other events, 8.2 us)
Sparse Core Ops, SparseCore 0:
  79.7 98.3 all-reduce.1
Sparse Core Ops, SparseCore 1:
  82.9 16.6 reduce-scatter.1
where the time goes:
time: 188 us
  waiting for transfers between devices  99.4 us (53%)
  starting transfers between devices  22.5 us (12%)
  local copies, waits for them, and re-layouts  18.3 us (10%)
  matrix products  17.7 us (9%)
  between operations  17.3 us (9%)
  loops' own time  10.7 us (6%)
  other arithmetic  2.13 us (1%)
    psum x1, waiting for transfers between devices, shards(): lax.psum(lax.dot_general(score_tokens, both_grads, over_rows, preferred_e...  94.5 us
    ppermute x8, starting transfers between devices, from_behind(): lax.ppermute(value, axis, [(source, source + steps) for source in range(f...  22.4 us
    unnamed x41, local copies, waits for them, and re-layouts  8.56 us
    another operation x3, loops' own time, shards(): lax.cond(live_flags[slot_index], backward_tile, empty_tile)  5.41 us
    another operation x3, loops' own time, shards(): lax.cond(live_flags[slot_index], lambda: tile_logits(key_tile, slot_index...  5.24 us
    dot_general x3, matrix products, shards(): jnp.einsum('grfs,sgd->fgrd', (expo / row_total[..., None]).astype(jnp.bfl...  5.21 us
    another operation x3, local copies, waits for them, and re-layouts  5.2 us
    ppermute x8, waiting for transfers between devices, from_behind(): lax.ppermute(value, axis, [(source, source + steps) for source in range(f...  4.87 us
  transfers between devices with their start and end apart: 10, of which 3 were waited for; matrix products, arithmetic and copies ran while one was open for 3% of the time, Pallas kernels for 0%

commit v1 on v0

v1 whole, which is shorter than its diff:
```python
import functools

import jax
import jax.numpy as jnp
from jax import lax
from jax.experimental import pallas as pl
from jax.experimental.pallas import tpu as pltpu
from jax.sharding import PartitionSpec as P

HD = 64
MAXW = 3
SLOTS = 2 * MAXW - 1
SOFTCAP = 5.0
LOG2E = 1.4426950408889634
F32 = jnp.float32
BF16 = jnp.bfloat16
MESH = pl.DeviceIdType.MESH
NT = (((1,), (1,)), ((), ()))
NN = (((1,), (0,)), ((), ()))


def mm(a, b, dims=NN):
    return lax.dot_general(a, b, dims, preferred_element_type=F32)


def kernel(n, direct, *refs):
    (lo_ref, hi_ref, lead_ref, q_ref, st_ref, kw_ref, vw_ref, da_ref) = refs[:8]
    if direct:
        att_ref, dq_ref, dst_ref, gk_ref, gv_ref = refs[8:13]
        rest = refs[13:]
    else:
        att_ref, dq_ref, dst_ref, part_ref = refs[8:12]
        rest = refs[12:]
    (table, k2, v2, qt, dat, stt, padded, back, back_in, wcat, cat, peer_kv, send_half, recv_half,
     own_half, rs_in, kv_s, kv_r, bk_s, bk_r, w_s, w_r, m_s, m_r, c_s, c_r, rs_s, rs_r) = rest

    t = lax.axis_index("tm")
    m = lax.axis_index("mp")
    core = lax.rem(t, 2)
    chips = n // 2
    frames = q_ref.shape[0]
    heads_pairs = q_ref.shape[1] // 128
    sb = st_ref.shape[0]
    win = MAXW * sb
    half = dst_ref.shape[1]
    hops = [d for d in range(1 - MAXW, MAXW) if d != 0]

    barrier = pltpu.get_barrier_semaphore()
    for d in hops:

        @pl.when((t + d >= 0) & (t + d < n))
        def _():
            pl.semaphore_signal(barrier, inc=1, device_id=(t + d, m), device_id_type=MESH)

    pl.semaphore_signal(barrier, inc=1, device_id=(t, 1 - m), device_id_type=MESH)
    count = jnp.minimum(t, MAXW - 1) + jnp.minimum(n - 1 - t, MAXW - 1) + 1
    if direct:
        for j in range(1, chips):
            pl.semaphore_signal(
                barrier, inc=1, device_id=(lax.rem(t + 2 * j, n), m), device_id_type=MESH
            )
        count = count + (chips - 1)

    st = st_ref[...]
    table[MAXW - 1, :, :128] = mm(st, kw_ref[...]).astype(BF16)
    table[MAXW - 1, :, 128:] = mm(st, vw_ref[...]).astype(BF16)
    pl.semaphore_wait(barrier, count)

    def kv_copy(i, d):
        return pltpu.make_async_remote_copy(
            src_ref=table.at[MAXW - 1], dst_ref=table.at[MAXW - 1 - d],
            send_sem=kv_s.at[i], recv_sem=kv_r.at[i],
            device_id=(t + d, m), device_id_type=MESH)

    def back_copy(i, d):
        return pltpu.make_async_remote_copy(
            src_ref=back.at[i], dst_ref=back_in.at[i],
            send_sem=bk_s.at[i], recv_sem=bk_r.at[i],
            device_id=(t + d, m), device_id_type=MESH)

    def in_range(d):
        return (t + d >= 0) & (t + d < n)

    for i, d in enumerate(hops):
        pl.when(in_range(d))(lambda i=i, d=d: kv_copy(i, d).start())
    far = pl.multiple_of((1 - m) * half, half)
    near = pl.multiple_of(m * half, half)
    w_copies = []
    for i, w in enumerate((kw_ref, vw_ref)):
        w_copies.append(pltpu.make_async_remote_copy(
            src_ref=w.at[pl.ds(far, half)], dst_ref=wcat.at[2 + i],
            send_sem=w_s.at[i], recv_sem=w_r.at[i],
            device_id=(t, 1 - m), device_id_type=MESH))
        w_copies[-1].start()

    wcat[0] = kw_ref[pl.ds(near, half), :]
    wcat[1] = vw_ref[pl.ds(near, half), :]
    qt[...] = (q_ref[...] * jnp.asarray(0.125, BF16)).T
    dat[...] = da_ref[...].T
    stt[...] = st.T.reshape(stt.shape)
    for s in (0, 1, MAXW + 2, MAXW + 3):
        padded[s] = jnp.zeros(padded.shape[1:], F32)
    for i, d in enumerate(hops):

        @pl.when(~in_range(-d))
        def _(i=i, d=d):
            table[MAXW - 1 - d] = jnp.zeros(table.shape[1:], BF16)
            back_in[i] = jnp.zeros(back_in.shape[1:], BF16)

    for i, d in enumerate(hops):
        pl.when(in_range(-d))(lambda i=i, d=d: kv_copy(i, d).wait_recv())

    lo, hi, lead = lo_ref[0], hi_ref[0], lead_ref[0]
    base = jnp.clip(lo - t + MAXW - 1, 0, MAXW - 1)
    for s in range(MAXW):
        tile = table[base + s].astype(F32)
        lane = lax.broadcasted_iota(jnp.int32, (sb, 128), 1)
        left = lane < HD
        for out, straight in ((k2, tile[:, :128]), (v2, tile[:, 128:])):
            swapped = pltpu.roll(straight, HD, 1)
            for g, (a, b) in enumerate(((straight, swapped), (swapped, straight))):
                out[g, s * sb:(s + 1) * sb] = jnp.where(left, a, 0.0).astype(BF16)
                out[g, win + s * sb:win + (s + 1) * sb] = jnp.where(left, 0.0, b).astype(BF16)

    column = lax.broadcasted_iota(jnp.int32, (1, win), 1)
    allowed = (column >= lead) & (column < (hi - lo) * sb)
    first = lax.broadcasted_iota(jnp.int32, (frames, 128), 1) < HD
    grads = [[None, None], [None, None]]
    for j in range(heads_pairs):
        g = j // 2
        cols = slice(128 * j, 128 * j + 128)
        qp = q_ref[:, cols] * jnp.asarray(0.125, BF16)
        dap = da_ref[:, cols]
        raw = mm(qp, k2[g], NT)
        d_probs = mm(dap, v2[g], NT)
        capped, probs, low = [], [], []
        for h in range(2):
            c = jnp.tanh(raw[:, h * win:(h + 1) * win] * (1.0 / SOFTCAP))
            e = jnp.where(allowed, jnp.exp2(c * (SOFTCAP * LOG2E)), 0.0)
            p = e * (1.0 / jnp.sum(e, -1, keepdims=True))
            capped.append(c)
            probs.append(p)
            low.append(p.astype(BF16))
        mixed = mm(low[0], v2[g, :win]) + mm(low[1], v2[g, win:])
        att_ref[:, cols] = mixed.astype(BF16)
        prod = mixed * dap.astype(F32)
        delta = [
            jnp.sum(jnp.where(first, prod, 0.0), -1, keepdims=True),
            jnp.sum(jnp.where(first, 0.0, prod), -1, keepdims=True),
        ]
        d_raw = []
        for h in range(2):
            c = capped[h]
            d_raw.append(
                (probs[h] * (d_probs[:, h * win:(h + 1) * win] - delta[h]) * (1.0 - c * c)).astype(BF16)
            )
        dqp = mm(d_raw[0], k2[g, :win]) + mm(d_raw[1], k2[g, win:])
        dq_ref[:, cols] = (dqp * 0.125).astype(BF16)
        for h in range(2):
            rows = slice((2 * j + h) * HD, (2 * j + h + 1) * HD)
            for which, (a, b) in enumerate(((qt, d_raw[h]), (dat, low[h]))):
                term = mm(a[rows, :], b)
                old = grads[which][g]
                grads[which][g] = term if old is None else old + term
    grad_t = jnp.concatenate([grads[0][0], grads[0][1], grads[1][0], grads[1][1]], 0)
    grad = grad_t.T
    for s in range(MAXW):
        padded[2 + s] = grad[s * sb:(s + 1) * sb]
    for i, d in enumerate(hops):
        back[i] = padded[d + (MAXW - 1) - base + 2].astype(BF16)
        pl.when(in_range(d))(lambda i=i, d=d: back_copy(i, d).start())
    total = padded[(MAXW - 1) - base + 2]
    for i, d in enumerate(hops):
        pl.when(in_range(-d))(lambda i=i, d=d: back_copy(i, d).wait_recv())
    for i, d in enumerate(hops):
        total = total + back_in[i].astype(F32)
    own_kv = total.astype(BF16)
    cat[...] = own_kv
    m_copy = pltpu.make_async_remote_copy(
        src_ref=cat, dst_ref=peer_kv, send_sem=m_s, recv_sem=m_r,
        device_id=(t, 1 - m), device_id_type=MESH)
    m_copy.start()

    if direct:
        rows = stt.shape[2]
        other = 1 - core
        c_copy = pltpu.make_async_remote_copy(
            src_ref=send_half, dst_ref=recv_half, send_sem=c_s, recv_sem=c_r,
            device_id=(t + 1 - 2 * core, m), device_id_type=MESH)
        lhs = stt[:, other].reshape(chips * rows, sb)
        send_half[...] = mm(lhs, own_kv).astype(BF16).reshape(send_half.shape)
        c_copy.start()
        lhs = stt[:, core].reshape(chips * rows, sb)
        mine = mm(lhs, own_kv).reshape(send_half.shape)
        c_copy.wait_recv()
        own_half[...] = (mine + recv_half[...].astype(F32)).astype(BF16)
        rs_copies = []
        for j in range(1, chips):
            target = lax.rem(t + 2 * j, n)
            rs_copies.append(pltpu.make_async_remote_copy(
                src_ref=own_half.at[lax.div(target, 2)], dst_ref=rs_in.at[j - 1],
                send_sem=rs_s.at[j - 1], recv_sem=rs_r.at[j - 1],
                device_id=(target, m), device_id_type=MESH))
            rs_copies[-1].start()
    else:
        part_ref[...] = mm(stt[...].reshape(part_ref.shape[0], sb), own_kv)

    for copy in w_copies:
        copy.wait_recv()
    term = mm(own_kv[:, :128], wcat[0], NT) + mm(own_kv[:, 128:], wcat[1], NT)
    m_copy.wait_recv()
    term = term + mm(peer_kv[:, :128], wcat[2], NT) + mm(peer_kv[:, 128:], wcat[3], NT)
    dst_ref[...] = term.astype(BF16)

    if direct:
        acc = own_half[lax.div(t, 2)].astype(F32)
        for j in range(1, chips):
            rs_copies[j - 1].wait_recv()
            acc = acc + rs_in[j - 1].astype(F32)
        gk_ref[...] = acc[:, :128]
        gv_ref[...] = acc[:, 128:]
        c_copy.wait_send()
        for copy in rs_copies:
            copy.wait_send()
    m_copy.wait_send()
    for copy in w_copies:
        copy.wait_send()
    for i, d in enumerate(hops):

        @pl.when(in_range(d))
        def _(i=i, d=d):
            kv_copy(i, d).wait_send()
            back_copy(i, d).wait_send()


def shards(n, queries, score_tokens, key_weight, value_weight, d_attended, band_lo, band_hi, lead):
    frames, width = queries.shape
    sb, model = score_tokens.shape
    half = model // lax.axis_size("mp")
    rows = model // n
    direct = n == 16
    cols = 2 * key_weight.shape[1]
    win = MAXW * sb
    chips = 8
    brow = model // 16
    outs = [
        jax.ShapeDtypeStruct((frames, width), BF16),
        jax.ShapeDtypeStruct((frames, width), BF16),
        jax.ShapeDtypeStruct((sb, half), BF16),
    ]
    if direct:
        outs += [jax.ShapeDtypeStruct((rows, cols // 2), F32)] * 2
    else:
        outs += [jax.ShapeDtypeStruct((model, cols), F32)]
    dma = pltpu.SemaphoreType.DMA
    vmem = pl.BlockSpec(memory_space=pltpu.VMEM)
    smem = pl.BlockSpec(memory_space=pltpu.SMEM)
    out = pl.pallas_call(
        functools.partial(kernel, n, direct),
        out_shape=outs,
        in_specs=[smem] * 3 + [vmem] * 5,
        out_specs=[vmem] * len(outs),
        scratch_shapes=[
            pltpu.VMEM((SLOTS, sb, cols), BF16),
            pltpu.VMEM((2, 2 * win, 128), BF16),
            pltpu.VMEM((2, 2 * win, 128), BF16),
            pltpu.VMEM((width, frames), BF16),
            pltpu.VMEM((width, frames), BF16),
            pltpu.VMEM((chips, 2, brow, sb), BF16),
            pltpu.VMEM((MAXW + 4, sb, cols), F32),
            pltpu.VMEM((SLOTS - 1, sb, cols), BF16),
            pltpu.VMEM((SLOTS - 1, sb, cols), BF16),
            pltpu.VMEM((4, half, cols // 2), BF16),
            pltpu.VMEM((sb, cols), BF16),
            pltpu.VMEM((sb, cols), BF16),
            pltpu.VMEM((chips, brow, cols), BF16),
            pltpu.VMEM((chips, brow, cols), BF16),
            pltpu.VMEM((chips, brow, cols), BF16),
            pltpu.VMEM((chips - 1, brow, cols), BF16),
            dma((SLOTS - 1,)),
            dma((SLOTS - 1,)),
            dma((SLOTS - 1,)),
            dma((SLOTS - 1,)),
            dma((2,)),
            dma((2,)),
            dma,
            dma,
            dma,
            dma,
            dma((chips - 1,)),
            dma((chips - 1,)),
        ],
        compiler_params=pltpu.CompilerParams(
            collective_id=0, has_side_effects=True, vmem_limit_bytes=40 * 1024 * 1024
        ),
        cost_estimate=pl.CostEstimate(
            flops=2_000_000_000, bytes_accessed=4_000_000, transcendentals=1_600_000
        ),
    )(band_lo, band_hi, lead, queries, score_tokens, key_weight, value_weight, d_attended)
    if direct:
        return tuple(out)
    attended, d_queries, d_score_tokens, part = out
    own = lax.psum_scatter(part, "tm", scatter_dimension=0, tiled=True)
    return attended, d_queries, d_score_tokens, own[:, : cols // 2], own[:, cols // 2 :]


def solution(mesh):
    in_specs = (
        P("tm", "mp"),
        P("tm", None),
        P(None, "mp"),
        P(None, "mp"),
        P("tm", "mp"),
        P("tm"),
        P("tm"),
        P("tm"),
    )
    out_specs = (P("tm", "mp"),) * 5
    return jax.shard_map(
        functools.partial(shards, mesh.shape["tm"]),
        mesh=mesh, in_specs=in_specs, out_specs=out_specs, check_vma=False)
```

time: 188 us -> 38.9 us (0.21)
  waiting for transfers between devices: 99.4 us -> 0 us
  Pallas kernels: 0 us -> 28 us
  starting transfers between devices: 22.5 us -> 0 us
  matrix products: 17.7 us -> 0 us
  between operations: 17.3 us -> 2.59 us
  loops' own time: 10.7 us -> 0 us
  local copies, waits for them, and re-layouts: 18.3 us -> 8.03 us
  other arithmetic: 2.13 us -> 0 us
    psum x1 -> x0, waiting for transfers between devices: 94.5 us -> none  [shards(): lax.psum(lax.dot_general(score_tokens, both_grads, over_rows, preferred_e...]
    pallas_call x0 -> x1, Pallas kernels: none -> 28 us  [shards(): pl.pallas_call(functools.partial(kernel, n, direct), out_shape=outs, in_s...]
    ppermute x8 -> x0, starting transfers between devices: 22.4 us -> none  [from_behind(): lax.ppermute(value, axis, [(source, source + steps) for source in range(f...]
    dot_general x26 -> x0, matrix products: 17.7 us -> none  [the longest x3 5.21 us: shards(): jnp.einsum('grfs,sgd->fgrd', (expo / row_total[..., None]).astype(jnp.bfl...]
    another operation x9 -> x0, loops' own time: 10.7 us -> none  [the longest x3 5.41 us: shards(): lax.cond(live_flags[slot_index], backward_tile, empty_tile)]
    another operation x4 -> x0, local copies, waits for them, and re-layouts: 5.21 us -> none
    ppermute x8 -> x0, waiting for transfers between devices: 4.87 us -> none  [from_behind(): lax.ppermute(value, axis, [(source, source + steps) for source in range(f...]
    cond x16 -> x0, local copies, waits for them, and re-layouts: 3.43 us -> none
  transfers between devices with their start and end apart: 10 -> 0, of which waited for: 3 -> 0; matrix products, arithmetic and copies ran while one was open for 3% -> 0% of each run, Pallas kernels for 0% -> 0%
where the time goes in v1:
time: 38.9 us; the launch traced here: 38.6 us
  Pallas kernels  28 us (72%)
  local copies, waits for them, and re-layouts  8.03 us (21%)
  between operations  2.59 us (7%)
    pallas_call x1, Pallas kernels, shards(): pl.pallas_call(functools.partial(kernel, n, direct), out_shape=outs, in_s...  28 us
    unnamed x15, local copies, waits for them, and re-layouts  8.03 us

profile of v1, /device:TPU:0, one launch (start us, length us, event | category | flops | bytes accessed | tf_op | source)
XLA Modules:
  0.0 38.6 jit_solution(15903148843401726269)
XLA Ops:
  2.6 0.0 copy-start
  2.6 0.9 %copy-done = bf16[256,512]{1,0:T(8,128)(2,1)S(1)} copy-done((bf16[256,512]{1,0:T(8,128)(2,1)S(1)}, bf16[256,512]{1,0:T(8,128)(2,1)}, u32[]{:S(2)}) %copy-start) | copy-done | bytes 262168
  3.5 0.0 copy-start.1
  3.5 0.9 %copy-done.1 = bf16[128,1024]{1,0:T(8,128)(2,1)S(1)} copy-done((bf16[128,1024]{1,0:T(8,128)(2,1)S(1)}, bf16[128,1024]{1,0:T(8,128)(2,1)}, u32[]{:S(2)}) %copy-start.1) | copy-done | bytes 262168
  4.5 0.0 copy-start.2
  4.5 0.9 %copy-done.2 = bf16[1024,128]{1,0:T(8,128)(2,1)S(1)} copy-done((bf16[1024,128]{1,0:T(8,128)(2,1)S(1)}, bf16[1024,128]{1,0:T(8,128)(2,1)}, u32[]{:S(2)}) %copy-start.2) | copy-done | bytes 262168
  5.4 0.0 copy-start.3
  5.4 0.9 %copy-done.3 = bf16[1024,128]{1,0:T(8,128)(2,1)S(1)} copy-done((bf16[1024,128]{1,0:T(8,128)(2,1)S(1)}, bf16[1024,128]{1,0:T(8,128)(2,1)}, u32[]{:S(2)}) %copy-start.3) | copy-done | bytes 262168
  6.4 0.0 copy-start.4
  6.4 0.9 %copy-done.4 = bf16[256,512]{1,0:T(8,128)(2,1)S(1)} copy-done((bf16[256,512]{1,0:T(8,128)(2,1)S(1)}, bf16[256,512]{1,0:T(8,128)(2,1)}, u32[]{:S(2)}) %copy-start.4) | copy-done | bytes 262168
  7.3 28.0 %shard_map.119 = (bf16[256,512]{1,0:T(8,128)(2,1)S(1)}, bf16[256,512]{1,0:T(8,128)(2,1)S(1)}, bf16[128,512]{1,0:T(8,128)(2,1)S(1)}, f32[64,128]{1,0:T(8,128)S(1)}, f32[64,128]{1,0:T(8,128)S(1)}) custom-call(s32[1]{0:T(128)S(6)} %copy.18.refs_0_, s32[1]{0:T(128)S(6)} %copy.19.refs_1_, s32[1]{0:T(128)S(6)} %copy.20.refs_2_, bf16[256,512]{1,0:T(8,128)(2,1)S(1)} %copy-done, ...), custom_call_target="tpu_custom_call" | custom-call | flops 2000000000 | bytes 4000000 | tf_op jit(solution)/shard_map/pallas_call | solution.py:258
  35.3 0.7 %copy.21 = bf16[256,512]{1,0:T(8,128)(2,1)} copy(bf16[256,512]{1,0:T(8,128)(2,1)S(1)} %get-tuple-element.10) | data formatting | bytes 524288
  36.0 0.7 %copy.22 = bf16[256,512]{1,0:T(8,128)(2,1)} copy(bf16[256,512]{1,0:T(8,128)(2,1)S(1)} %get-tuple-element.11) | data formatting | bytes 524288
  36.7 0.7 %copy.23 = bf16[128,512]{1,0:T(8,128)(2,1)} copy(bf16[128,512]{1,0:T(8,128)(2,1)S(1)} %get-tuple-element.12) | data formatting | bytes 262144
  37.4 0.6 %copy.24 = f32[64,128]{1,0:T(8,128)} copy(f32[64,128]{1,0:T(8,128)S(1)} %get-tuple-element.13) | data formatting | bytes 65536
  38.0 0.6 %copy.25 = f32[64,128]{1,0:T(8,128)} copy(f32[64,128]{1,0:T(8,128)S(1)} %get-tuple-element.14) | data formatting | bytes 65536
Async XLA Ops:
  2.6 1.0 %copy-start = (bf16[256,512]{1,0:T(8,128)(2,1)S(1)}, bf16[256,512]{1,0:T(8,128)(2,1)}, u32[]{:S(2)}) copy-start(bf16[256,512]{1,0:T(8,128)(2,1)} %refs_3_.1) | copy-start | bytes 786436
  3.5 0.9 %copy-start.1 = (bf16[128,1024]{1,0:T(8,128)(2,1)S(1)}, bf16[128,1024]{1,0:T(8,128)(2,1)}, u32[]{:S(2)}) copy-start(bf16[128,1024]{1,0:T(8,128)(2,1)} %refs_4_.1) | copy-start | bytes 786436
  4.5 0.9 %copy-start.2 = (bf16[1024,128]{1,0:T(8,128)(2,1)S(1)}, bf16[1024,128]{1,0:T(8,128)(2,1)}, u32[]{:S(2)}) copy-start(bf16[1024,128]{1,0:T(8,128)(2,1)} %refs_5_.1) | copy-start | bytes 786436
  5.4 0.9 %copy-start.3 = (bf16[1024,128]{1,0:T(8,128)(2,1)S(1)}, bf16[1024,128]{1,0:T(8,128)(2,1)}, u32[]{:S(2)}) copy-start(bf16[1024,128]{1,0:T(8,128)(2,1)} %refs_6_.1) | copy-start | bytes 786436
  6.4 0.9 %copy-start.4 = (bf16[256,512]{1,0:T(8,128)(2,1)S(1)}, bf16[256,512]{1,0:T(8,128)(2,1)}, u32[]{:S(2)}) copy-start(bf16[256,512]{1,0:T(8,128)(2,1)} %refs_7_.1) | copy-start | bytes 786436

commit v2 on v1

v2 whole, which is shorter than its diff:
```python
import functools

import jax
import jax.numpy as jnp
from jax import lax
from jax.experimental import pallas as pl
from jax.experimental.pallas import tpu as pltpu
from jax.sharding import PartitionSpec as P

HD = 64
MAXW = 3
SLOTS = 2 * MAXW - 1
SOFTCAP = 5.0
LOG2E = 1.4426950408889634
VMEM_LIMIT = 60 * 1024 * 1024
F32 = jnp.float32
BF16 = jnp.bfloat16
MESH = pl.DeviceIdType.MESH
NT = (((1,), (1,)), ((), ()))
NN = (((1,), (0,)), ((), ()))


def mm(a, b, dims=NN):
    return lax.dot_general(a, b, dims, preferred_element_type=F32)


def kernel(n, direct, *refs):
    (lo_ref, hi_ref, lead_ref, q_hbm, st_hbm, kw_hbm, vw_hbm, da_hbm) = refs[:8]
    if direct:
        out_hbm, rest = refs[8:13], refs[13:]
        att_ref, dq_ref, dst_ref, gk_ref, gv_ref, out_s = rest[:6]
        rest = rest[6:]
    else:
        out_hbm, rest = refs[8:12], refs[12:]
        att_ref, dq_ref, dst_ref, part_ref, out_s = rest[:5]
        rest = rest[5:]
    (q_ref, st_ref, kw_ref, vw_ref, da_ref, table, k2, v2, qt, dat, stt, padded, back, back_in, wcat,
     cat, peer_kv, send_half, recv_half, own_half, rs_in, in_s, kv_s, kv_r, bk_s, bk_r, w_s, w_r,
     m_s, m_r, c_s, c_r, rs_s, rs_r) = rest

    t = lax.axis_index("tm")
    m = lax.axis_index("mp")
    core = lax.rem(t, 2)
    chips = n // 2
    frames = q_ref.shape[0]
    sb = st_ref.shape[0]
    win = MAXW * sb
    half = dst_ref.shape[1]
    hops = [d for d in range(1 - MAXW, MAXW) if d != 0]

    def in_range(d):
        return (t + d >= 0) & (t + d < n)

    loads = [
        pltpu.make_async_copy(a, b, in_s.at[i])
        for i, (a, b) in enumerate(
            ((st_hbm, st_ref), (kw_hbm, kw_ref), (vw_hbm, vw_ref), (q_hbm, q_ref), (da_hbm, da_ref)))
    ]
    for load in loads:
        load.start()

    kept = (att_ref, dq_ref, dst_ref) + ((gk_ref, gv_ref) if direct else (part_ref,))
    stores = [
        pltpu.make_async_copy(a, b, out_s.at[i]) for i, (a, b) in enumerate(zip(kept, out_hbm))
    ]

    barrier = pltpu.get_barrier_semaphore()
    for d in hops:

        @pl.when(in_range(d))
        def _(d=d):
            pl.semaphore_signal(barrier, inc=1, device_id=(t + d, m), device_id_type=MESH)

    pl.semaphore_signal(barrier, inc=1, device_id=(t, 1 - m), device_id_type=MESH)
    count = jnp.minimum(t, MAXW - 1) + jnp.minimum(n - 1 - t, MAXW - 1) + 1
    if direct:
        for j in range(1, chips):
            pl.semaphore_signal(
                barrier, inc=1, device_id=(lax.rem(t + 2 * j, n), m), device_id_type=MESH
            )
        count = count + (chips - 1)

    for load in loads[:3]:
        load.wait()
    st = st_ref[...]
    table[MAXW - 1, :, :128] = mm(st, kw_ref[...]).astype(BF16)
    table[MAXW - 1, :, 128:] = mm(st, vw_ref[...]).astype(BF16)
    pl.semaphore_wait(barrier, count)

    def kv_copy(i, d):
        return pltpu.make_async_remote_copy(
            src_ref=table.at[MAXW - 1], dst_ref=table.at[MAXW - 1 - d],
            send_sem=kv_s.at[i], recv_sem=kv_r.at[i],
            device_id=(t + d, m), device_id_type=MESH)

    def back_copy(g, i, d):
        return pltpu.make_async_remote_copy(
            src_ref=back.at[g, i], dst_ref=back_in.at[g, i],
            send_sem=bk_s.at[g, i], recv_sem=bk_r.at[g, i],
            device_id=(t + d, m), device_id_type=MESH)

    for i, d in enumerate(hops):
        pl.when(in_range(d))(lambda i=i, d=d: kv_copy(i, d).start())
    far = pl.multiple_of((1 - m) * half, half)
    near = pl.multiple_of(m * half, half)
    w_copies = []
    for i, w in enumerate((kw_ref, vw_ref)):
        w_copies.append(pltpu.make_async_remote_copy(
            src_ref=w.at[pl.ds(far, half)], dst_ref=wcat.at[2 + i],
            send_sem=w_s.at[i], recv_sem=w_r.at[i],
            device_id=(t, 1 - m), device_id_type=MESH))
        w_copies[-1].start()

    for load in loads[3:]:
        load.wait()
    wcat[0] = kw_ref[pl.ds(near, half), :]
    wcat[1] = vw_ref[pl.ds(near, half), :]
    qt[...] = (q_ref[...] * jnp.asarray(0.125, BF16)).T
    dat[...] = da_ref[...].T
    stt[...] = st.T.reshape(stt.shape)
    for s in (0, 1, MAXW + 2, MAXW + 3):
        padded[:, s] = jnp.zeros((2,) + padded.shape[2:], F32)
    for i, d in enumerate(hops):

        @pl.when(~in_range(-d))
        def _(i=i, d=d):
            table[MAXW - 1 - d] = jnp.zeros(table.shape[1:], BF16)
            back_in[:, i] = jnp.zeros((2,) + back_in.shape[2:], BF16)

    for i, d in enumerate(hops):
        pl.when(in_range(-d))(lambda i=i, d=d: kv_copy(i, d).wait_recv())

    lo, hi, lead = lo_ref[0], hi_ref[0], lead_ref[0]
    base = jnp.clip(lo - t + MAXW - 1, 0, MAXW - 1)
    for s in range(MAXW):
        tile = table[base + s].astype(F32)
        lane = lax.broadcasted_iota(jnp.int32, (sb, 128), 1)
        left = lane < HD
        for out, straight in ((k2, tile[:, :128]), (v2, tile[:, 128:])):
            swapped = pltpu.roll(straight, HD, 1)
            for g, (a, b) in enumerate(((straight, swapped), (swapped, straight))):
                out[g, s * sb:(s + 1) * sb] = jnp.where(left, a, 0.0).astype(BF16)
                out[g, win + s * sb:win + (s + 1) * sb] = jnp.where(left, 0.0, b).astype(BF16)

    column = lax.broadcasted_iota(jnp.int32, (1, win), 1)
    allowed = (column >= lead) & (column < (hi - lo) * sb)
    first = lax.broadcasted_iota(jnp.int32, (frames, 128), 1) < HD

    def attend(j, grads):
        g = j // 2
        cols = slice(128 * j, 128 * j + 128)
        qp = q_ref[:, cols] * jnp.asarray(0.125, BF16)
        dap = da_ref[:, cols]
        raw = mm(qp, k2[g], NT)
        d_probs = mm(dap, v2[g], NT)
        capped, probs, low = [], [], []
        for h in range(2):
            c = jnp.tanh(raw[:, h * win:(h + 1) * win] * (1.0 / SOFTCAP))
            e = jnp.where(allowed, jnp.exp2(c * (SOFTCAP * LOG2E)), 0.0)
            p = e * (1.0 / jnp.sum(e, -1, keepdims=True))
            capped.append(c)
            probs.append(p)
            low.append(p.astype(BF16))
        mixed = mm(low[0], v2[g, :win]) + mm(low[1], v2[g, win:])
        att_ref[:, cols] = mixed.astype(BF16)
        prod = mixed * dap.astype(F32)
        delta = [
            jnp.sum(jnp.where(first, prod, 0.0), -1, keepdims=True),
            jnp.sum(jnp.where(first, 0.0, prod), -1, keepdims=True),
        ]
        d_raw = []
        for h in range(2):
            c = capped[h]
            d_raw.append(
                (probs[h] * (d_probs[:, h * win:(h + 1) * win] - delta[h]) * (1.0 - c * c)).astype(BF16)
            )
        dqp = mm(d_raw[0], k2[g, :win]) + mm(d_raw[1], k2[g, win:])
        dq_ref[:, cols] = (dqp * 0.125).astype(BF16)
        grads = list(grads)
        for h in range(2):
            rows = slice((2 * j + h) * HD, (2 * j + h + 1) * HD)
            for which, (a, b) in enumerate(((qt, d_raw[h]), (dat, low[h]))):
                term = mm(a[rows, :], b)
                grads[which] = term if grads[which] is None else grads[which] + term
        return grads

    def send_back(g, grads):
        grad = jnp.concatenate(grads, 0).T
        for s in range(MAXW):
            padded[g, 2 + s] = grad[s * sb:(s + 1) * sb]
        for i, d in enumerate(hops):
            back[g, i] = padded[g, d + (MAXW - 1) - base + 2].astype(BF16)
            pl.when(in_range(d))(lambda i=i, d=d: back_copy(g, i, d).start())

    m_copies = [
        pltpu.make_async_remote_copy(
            src_ref=cat.at[g], dst_ref=peer_kv.at[g], send_sem=m_s.at[g], recv_sem=m_r.at[g],
            device_id=(t, 1 - m), device_id_type=MESH)
        for g in range(2)
    ]
    rows = stt.shape[2]
    if direct:
        c_copies = [
            pltpu.make_async_remote_copy(
                src_ref=send_half.at[g], dst_ref=recv_half.at[g],
                send_sem=c_s.at[g], recv_sem=c_r.at[g],
                device_id=(t + 1 - 2 * core, m), device_id_type=MESH)
            for g in range(2)
        ]

        def rs_copy(g, j):
            target = lax.rem(t + 2 * j, n)
            return pltpu.make_async_remote_copy(
                src_ref=own_half.at[g, lax.div(target, 2)], dst_ref=rs_in.at[g, j - 1],
                send_sem=rs_s.at[g, j - 1], recv_sem=rs_r.at[g, j - 1],
                device_id=(target, m), device_id_type=MESH)

    def collect(g):
        total = padded[g, (MAXW - 1) - base + 2]
        for i, d in enumerate(hops):
            pl.when(in_range(-d))(lambda i=i, d=d: back_copy(g, i, d).wait_recv())
        for i, d in enumerate(hops):
            total = total + back_in[g, i].astype(F32)
        own = total.astype(BF16)
        cat[g] = own
        m_copies[g].start()
        if direct:
            lhs = stt[:, 1 - core].reshape(chips * rows, sb)
            send_half[g] = mm(lhs, own).astype(BF16).reshape(send_half.shape[1:])
            c_copies[g].start()
            lhs = stt[:, core].reshape(chips * rows, sb)
            return mm(lhs, own).reshape(send_half.shape[1:])
        part_ref[:, 128 * g:128 * g + 128] = mm(stt[...].reshape(part_ref.shape[0], sb), own)
        return None

    def spread(g, mine):
        if direct:
            c_copies[g].wait_recv()
            own_half[g] = (mine + recv_half[g].astype(F32)).astype(BF16)
            for j in range(1, chips):
                rs_copy(g, j).start()

    def by_kind(a):
        pieces = [a[0], a[1]]
        return [
            jnp.concatenate([p[:, HD * which:HD * which + HD] for p in pieces], 1)
            for which in range(2)
        ]

    grads = attend(1, attend(0, [None, None]))
    send_back(0, grads)
    grads = attend(2, [None, None])
    mine = collect(0)
    grads = attend(3, grads)
    spread(0, mine)
    send_back(1, grads)
    stores[0].start()
    stores[1].start()
    mine = collect(1)
    for copy in w_copies:
        copy.wait_recv()
    keys, values = by_kind(cat)
    term = mm(keys, wcat[0], NT) + mm(values, wcat[1], NT)
    spread(1, mine)
    for copy in m_copies:
        copy.wait_recv()
    keys, values = by_kind(peer_kv)
    term = term + mm(keys, wcat[2], NT) + mm(values, wcat[3], NT)
    dst_ref[...] = term.astype(BF16)
    stores[2].start()

    if direct:
        sums = []
        for g in range(2):
            acc = own_half[g, lax.div(t, 2)].astype(F32)
            for j in range(1, chips):
                rs_copy(g, j).wait_recv()
                acc = acc + rs_in[g, j - 1].astype(F32)
            sums.append(acc)
        gk_ref[...], gv_ref[...] = by_kind(sums)
        stores[3].start()
        stores[4].start()
        for g in range(2):
            c_copies[g].wait_send()
            for j in range(1, chips):
                rs_copy(g, j).wait_send()
    else:
        stores[3].start()
    for copy in m_copies + w_copies:
        copy.wait_send()
    for i, d in enumerate(hops):

        @pl.when(in_range(d))
        def _(i=i, d=d):
            kv_copy(i, d).wait_send()
            for g in range(2):
                back_copy(g, i, d).wait_send()

    for store in stores:
        store.wait()


def place(*refs):
    count = (len(refs) - 1) // 2
    copies = [
        pltpu.make_async_copy(refs[i], refs[count + i], refs[-1].at[i]) for i in range(count)
    ]
    for copy in copies:
        copy.start()
    for copy in copies:
        copy.wait()


def shards(n, queries, score_tokens, key_weight, value_weight, d_attended, band_lo, band_hi, lead):
    frames, width = queries.shape
    sb, model = score_tokens.shape
    half = model // lax.axis_size("mp")
    rows = model // n
    direct = n == 16
    cols = 2 * key_weight.shape[1]
    win = MAXW * sb
    chips = 8
    brow = model // 16
    outs = [
        jax.ShapeDtypeStruct((frames, width), BF16),
        jax.ShapeDtypeStruct((frames, width), BF16),
        jax.ShapeDtypeStruct((sb, half), BF16),
    ]
    if direct:
        outs += [jax.ShapeDtypeStruct((rows, cols // 2), F32)] * 2
    else:
        outs += [jax.ShapeDtypeStruct((model, cols), F32)]
    dma = pltpu.SemaphoreType.DMA
    smem = pl.BlockSpec(memory_space=pltpu.SMEM)
    hbm = pl.BlockSpec(memory_space=pltpu.HBM)
    pair = cols // 2
    out = pl.pallas_call(
        functools.partial(kernel, n, direct),
        out_shape=outs,
        in_specs=[smem] * 3 + [hbm] * 5,
        out_specs=[hbm] * len(outs),
        scratch_shapes=[pltpu.VMEM(o.shape, o.dtype) for o in outs] + [
            dma((len(outs),)),
            pltpu.VMEM((frames, width), BF16),
            pltpu.VMEM((sb, model), BF16),
            pltpu.VMEM((model, pair), BF16),
            pltpu.VMEM((model, pair), BF16),
            pltpu.VMEM((frames, width), BF16),
            pltpu.VMEM((SLOTS, sb, cols), BF16),
            pltpu.VMEM((2, 2 * win, 128), BF16),
            pltpu.VMEM((2, 2 * win, 128), BF16),
            pltpu.VMEM((width, frames), BF16),
            pltpu.VMEM((width, frames), BF16),
            pltpu.VMEM((chips, 2, brow, sb), BF16),
            pltpu.VMEM((2, MAXW + 4, sb, pair), F32),
            pltpu.VMEM((2, SLOTS - 1, sb, pair), BF16),
            pltpu.VMEM((2, SLOTS - 1, sb, pair), BF16),
            pltpu.VMEM((4, half, pair), BF16),
            pltpu.VMEM((2, sb, pair), BF16),
            pltpu.VMEM((2, sb, pair), BF16),
            pltpu.VMEM((2, chips, brow, pair), BF16),
            pltpu.VMEM((2, chips, brow, pair), BF16),
            pltpu.VMEM((2, chips, brow, pair), BF16),
            pltpu.VMEM((2, chips - 1, brow, pair), BF16),
            dma((5,)),
            dma((SLOTS - 1,)),
            dma((SLOTS - 1,)),
            dma((2, SLOTS - 1)),
            dma((2, SLOTS - 1)),
            dma((2,)),
            dma((2,)),
            dma((2,)),
            dma((2,)),
            dma((2,)),
            dma((2,)),
            dma((2, chips - 1)),
            dma((2, chips - 1)),
        ],
        compiler_params=pltpu.CompilerParams(
            collective_id=0, has_side_effects=True, vmem_limit_bytes=VMEM_LIMIT
        ),
        cost_estimate=pl.CostEstimate(
            flops=2_000_000_000, bytes_accessed=4_000_000, transcendentals=1_600_000
        ),
    )(band_lo, band_hi, lead, queries, score_tokens, key_weight, value_weight, d_attended)
    if direct:
        return tuple(
            pl.pallas_call(
                place,
                out_shape=outs,
                in_specs=[hbm] * len(outs),
                out_specs=[hbm] * len(outs),
                scratch_shapes=[dma((len(outs),))],
                compiler_params=pltpu.CompilerParams(vmem_limit_bytes=VMEM_LIMIT),
            )(*out)
        )
    attended, d_queries, d_score_tokens, part = out
    own = lax.psum_scatter(part, "tm", scatter_dimension=0, tiled=True)
    parts = own.reshape(rows, 2, 2, HD).transpose(2, 0, 1, 3).reshape(2, rows, cols // 2)
    return attended, d_queries, d_score_tokens, parts[0], parts[1]


def solution(mesh):
    in_specs = (
        P("tm", "mp"),
        P("tm", None),
        P(None, "mp"),
        P(None, "mp"),
        P("tm", "mp"),
        P("tm"),
        P("tm"),
        P("tm"),
    )
    out_specs = (P("tm", "mp"),) * 5
    return jax.shard_map(
        functools.partial(shards, mesh.shape["tm"]),
        mesh=mesh, in_specs=in_specs, out_specs=out_specs, check_vma=False)
```

time: 38.9 us -> 56.7 us (1.46)
  Pallas kernels: 28 us -> 54 us
  local copies, waits for them, and re-layouts: 8.03 us -> 0 us
    pallas_call x0 -> x1, Pallas kernels: none -> 23 us  [shards(): pl.pallas_call(place, out_shape=outs, in_specs=[hbm] * len(outs), out_spe...]
    unnamed x15 -> x0, local copies, waits for them, and re-layouts: 8.03 us -> none
    pallas_call x1, Pallas kernels: 28 us -> 31 us  [shards(): pl.pallas_call(functools.partial(kernel, n, direct), out_shape=outs, in_s...]
where the time goes in v2:
time: 56.7 us; the launch traced here: 56.6 us
  Pallas kernels  54 us (95%)
  between operations  2.58 us (5%)
    pallas_call x1, Pallas kernels, shards(): pl.pallas_call(functools.partial(kernel, n, direct), out_shape=outs, in_s...  31 us
    pallas_call x1, Pallas kernels, shards(): pl.pallas_call(place, out_shape=outs, in_specs=[hbm] * len(outs), out_spe...  23 us

profile of v2, /device:TPU:0, one launch (start us, length us, event | category | flops | bytes accessed | tf_op | source)
XLA Modules:
  0.0 56.6 jit_solution(14550492070335800242)
XLA Ops:
  2.6 31.0 %shard_map.119 = (bf16[256,512]{1,0:T(8,128)(2,1)}, bf16[256,512]{1,0:T(8,128)(2,1)}, bf16[128,512]{1,0:T(8,128)(2,1)}, f32[64,128]{1,0:T(8,128)}, f32[64,128]{1,0:T(8,128)}) custom-call(s32[1]{0:T(128)S(6)} %copy.13.refs_0_, s32[1]{0:T(128)S(6)} %copy.14.refs_1_, s32[1]{0:T(128)S(6)} %copy.15.refs_2_, bf16[256,512]{1,0:T(8,128)(2,1)} %refs_3_.1, ...), custom_call_target="tpu_custom_call" | custom-call | flops 2000000000 | bytes 4000000 | tf_op jit(solution)/shard_map/pallas_call | solution.py:337
  33.6 23.0 %shard_map.120 = (bf16[256,512]{1,0:T(8,128)(2,1)}, bf16[256,512]{1,0:T(8,128)(2,1)}, bf16[128,512]{1,0:T(8,128)(2,1)}, f32[64,128]{1,0:T(8,128)}, f32[64,128]{1,0:T(8,128)}) custom-call(bf16[256,512]{1,0:T(8,128)(2,1)} %get-tuple-element.10.refs_0_, bf16[256,512]{1,0:T(8,128)(2,1)} %get-tuple-element.11.refs_1_, ...), custom_call_target="tpu_custom_call" | custom-call | tf_op jit(solution)/shard_map/pallas_call | solution.py:388

commit v3 on v2

--- a/solution.py
+++ b/solution.py
@@ -34,14 +34,15 @@
         out_hbm, rest = refs[8:12], refs[12:]
         att_ref, dq_ref, dst_ref, part_ref, out_s = rest[:5]
         rest = rest[5:]
-    (q_ref, st_ref, kw_ref, vw_ref, da_ref, table, k2, v2, qt, dat, stt, padded, back, back_in, wcat,
-     cat, peer_kv, send_half, recv_half, own_half, rs_in, in_s, kv_s, kv_r, bk_s, bk_r, w_s, w_r,
+    (q_ref, st_ref, kw_ref, vw_ref, da_ref, table_a, table_b, k2, v2, qt, dat, stt, padded, back, back_in, wcat,
+     cat, peer_kv, chip_kv, stt_peer, own_half, rs_in, s_s, s_r, in_s, kv_s, kv_r, bk_s, bk_r, w_s, w_r,
      m_s, m_r, c_s, c_r, rs_s, rs_r) = rest
 
     t = lax.axis_index("tm")
     m = lax.axis_index("mp")
     core = lax.rem(t, 2)
     chips = n // 2
+    chips_cut = stt.shape[1]
     frames = q_ref.shape[0]
     sb = st_ref.shape[0]
     win = MAXW * sb
@@ -83,14 +84,18 @@
     for load in loads[:3]:
         load.wait()
     st = st_ref[...]
-    table[MAXW - 1, :, :128] = mm(st, kw_ref[...]).astype(BF16)
-    table[MAXW - 1, :, 128:] = mm(st, vw_ref[...]).astype(BF16)
+    tables = (table_a, table_b)
+    keys = mm(st, kw_ref[...])
+    values = mm(st, vw_ref[...])
+    for g in range(2):
+        lanes = slice(HD * g, HD * g + HD)
+        tables[g][MAXW - 1] = jnp.concatenate([keys[:, lanes], values[:, lanes]], 1).astype(BF16)
     pl.semaphore_wait(barrier, count)
 
-    def kv_copy(i, d):
+    def kv_copy(g, i, d):
         return pltpu.make_async_remote_copy(
-            src_ref=table.at[MAXW - 1], dst_ref=table.at[MAXW - 1 - d],
-            send_sem=kv_s.at[i], recv_sem=kv_r.at[i],
+            src_ref=tables[g].at[MAXW - 1], dst_ref=tables[g].at[MAXW - 1 - d],
+            send_sem=kv_s.at[g, i], recv_sem=kv_r.at[g, i],
             device_id=(t + d, m), device_id_type=MESH)
 
     def back_copy(g, i, d):
@@ -99,8 +104,9 @@
             send_sem=bk_s.at[g, i], recv_sem=bk_r.at[g, i],
             device_id=(t + d, m), device_id_type=MESH)
 
-    for i, d in enumerate(hops):
-        pl.when(in_range(d))(lambda i=i, d=d: kv_copy(i, d).start())
+    for g in range(2):
+        for i, d in enumerate(hops):
+            pl.when(in_range(d))(lambda g=g, i=i, d=d: kv_copy(g, i, d).start())
     far = pl.multiple_of((1 - m) * half, half)
     near = pl.multiple_of(m * half, half)
     w_copies = []
@@ -117,28 +123,33 @@
     wcat[1] = vw_ref[pl.ds(near, half), :]
     qt[...] = (q_ref[...] * jnp.asarray(0.125, BF16)).T
     dat[...] = da_ref[...].T
-    stt[...] = st.T.reshape(stt.shape)
+    stt[...] = jnp.swapaxes(st.T.reshape(chips_cut, 2, stt.shape[2], sb), 0, 1)
+    if direct:
+        s_copy = pltpu.make_async_remote_copy(
+            src_ref=stt.at[1 - core], dst_ref=stt_peer, send_sem=s_s, recv_sem=s_r,
+            device_id=(t + 1 - 2 * core, m), device_id_type=MESH)
+        s_copy.start()
     for s in (0, 1, MAXW + 2, MAXW + 3):
         padded[:, s] = jnp.zeros((2,) + padded.shape[2:], F32)
     for i, d in enumerate(hops):
 
         @pl.when(~in_range(-d))
         def _(i=i, d=d):
-            table[MAXW - 1 - d] = jnp.zeros(table.shape[1:], BF16)
+            for tab in tables:
+                tab[MAXW - 1 - d] = jnp.zeros(tab.shape[1:], BF16)
             back_in[:, i] = jnp.zeros((2,) + back_in.shape[2:], BF16)
-
-    for i, d in enumerate(hops):
-        pl.when(in_range(-d))(lambda i=i, d=d: kv_copy(i, d).wait_recv())
 
     lo, hi, lead = lo_ref[0], hi_ref[0], lead_ref[0]
     base = jnp.clip(lo - t + MAXW - 1, 0, MAXW - 1)
-    for s in range(MAXW):
-        tile = table[base + s].astype(F32)
-        lane = lax.broadcasted_iota(jnp.int32, (sb, 128), 1)
-        left = lane < HD
-        for out, straight in ((k2, tile[:, :128]), (v2, tile[:, 128:])):
-            swapped = pltpu.roll(straight, HD, 1)
-            for g, (a, b) in enumerate(((straight, swapped), (swapped, straight))):
+    left = lax.broadcasted_iota(jnp.int32, (sb, 128), 1) < HD
+
+    def unpack(g):
+        for i, d in enumerate(hops):
+            pl.when(in_range(-d))(lambda i=i, d=d: kv_copy(g, i, d).wait_recv())
+        for s in range(MAXW):
+            tile = tables[g][base + s].astype(F32)
+            swapped = pltpu.roll(tile, HD, 1)
+            for out, a, b in ((k2, tile, swapped), (v2, swapped, tile)):
                 out[g, s * sb:(s + 1) * sb] = jnp.where(left, a, 0.0).astype(BF16)
                 out[g, win + s * sb:win + (s + 1) * sb] = jnp.where(left, 0.0, b).astype(BF16)
 
@@ -202,7 +213,7 @@
     if direct:
         c_copies = [
             pltpu.make_async_remote_copy(
-                src_ref=send_half.at[g], dst_ref=recv_half.at[g],
+                src_ref=cat.at[g], dst_ref=chip_kv.at[g],
                 send_sem=c_s.at[g], recv_sem=c_r.at[g],
                 device_id=(t + 1 - 2 * core, m), device_id_type=MESH)
             for g in range(2)
@@ -225,18 +236,17 @@
         cat[g] = own
         m_copies[g].start()
         if direct:
-            lhs = stt[:, 1 - core].reshape(chips * rows, sb)
-            send_half[g] = mm(lhs, own).astype(BF16).reshape(send_half.shape[1:])
             c_copies[g].start()
-            lhs = stt[:, core].reshape(chips * rows, sb)
-            return mm(lhs, own).reshape(send_half.shape[1:])
-        part_ref[:, 128 * g:128 * g + 128] = mm(stt[...].reshape(part_ref.shape[0], sb), own)
+            return mm(stt[core].reshape(chips * rows, sb), own)
+        part_ref[:, 128 * g:128 * g + 128] = mm(
+            jnp.swapaxes(stt[...], 0, 1).reshape(part_ref.shape[0], sb), own)
         return None
 
     def spread(g, mine):
         if direct:
             c_copies[g].wait_recv()
-            own_half[g] = (mine + recv_half[g].astype(F32)).astype(BF16)
+            both = mine + mm(stt_peer[...].reshape(chips * rows, sb), chip_kv[g])
+            own_half[g] = both.astype(BF16).reshape(own_half.shape[1:])
             for j in range(1, chips):
                 rs_copy(g, j).start()
 
@@ -247,13 +257,16 @@
             for which in range(2)
         ]
 
+    unpack(0)
     grads = attend(1, attend(0, [None, None]))
     send_back(0, grads)
-    grads = attend(2, [None, None])
+    unpack(1)
+    grads = attend(3, attend(2, [None, None]))
+    send_back(1, grads)
+    if direct:
+        s_copy.wait_recv()
     mine = collect(0)
-    grads = attend(3, grads)
     spread(0, mine)
-    send_back(1, grads)
     stores[0].start()
     stores[1].start()
     mine = collect(1)
@@ -280,6 +293,7 @@
         gk_ref[...], gv_ref[...] = by_kind(sums)
         stores[3].start()
         stores[4].start()
+        s_copy.wait_send()
         for g in range(2):
             c_copies[g].wait_send()
             for j in range(1, chips):
@@ -292,8 +306,8 @@
 
         @pl.when(in_range(d))
         def _(i=i, d=d):
-            kv_copy(i, d).wait_send()
             for g in range(2):
+                kv_copy(g, i, d).wait_send()
                 back_copy(g, i, d).wait_send()
 
     for store in stores:
@@ -301,14 +315,18 @@
 
 
 def place(*refs):
-    count = (len(refs) - 1) // 2
-    copies = [
-        pltpu.make_async_copy(refs[i], refs[count + i], refs[-1].at[i]) for i in range(count)
-    ]
-    for copy in copies:
-        copy.start()
-    for copy in copies:
-        copy.wait()
+    count = (len(refs) - 2) // 3
+    sources, targets, held = (refs[i * count:(i + 1) * count] for i in range(3))
+    load_s, store_s = refs[-2:]
+    loads = [pltpu.make_async_copy(sources[i], held[i], load_s.at[i]) for i in range(count)]
+    stores = [pltpu.make_async_copy(held[i], targets[i], store_s.at[i]) for i in range(count)]
+    for load in loads:
+        load.start()
+    for load, store in zip(loads, stores):
+        load.wait()
+        store.start()
+    for store in stores:
+        store.wait()
 
 
 def shards(n, queries, score_tokens, key_weight, value_weight, d_attended, band_lo, band_hi, lead):
@@ -346,25 +364,28 @@
             pltpu.VMEM((model, pair), BF16),
             pltpu.VMEM((model, pair), BF16),
             pltpu.VMEM((frames, width), BF16),
-            pltpu.VMEM((SLOTS, sb, cols), BF16),
+            pltpu.VMEM((SLOTS, sb, pair), BF16),
+            pltpu.VMEM((SLOTS, sb, pair), BF16),
             pltpu.VMEM((2, 2 * win, 128), BF16),
             pltpu.VMEM((2, 2 * win, 128), BF16),
             pltpu.VMEM((width, frames), BF16),
             pltpu.VMEM((width, frames), BF16),
-            pltpu.VMEM((chips, 2, brow, sb), BF16),
+            pltpu.VMEM((2, chips, brow, sb), BF16),
             pltpu.VMEM((2, MAXW + 4, sb, pair), F32),
             pltpu.VMEM((2, SLOTS - 1, sb, pair), BF16),
             pltpu.VMEM((2, SLOTS - 1, sb, pair), BF16),
             pltpu.VMEM((4, half, pair), BF16),
             pltpu.VMEM((2, sb, pair), BF16),
             pltpu.VMEM((2, sb, pair), BF16),
-            pltpu.VMEM((2, chips, brow, pair), BF16),
-            pltpu.VMEM((2, chips, brow, pair), BF16),
+            pltpu.VMEM((2, sb, pair), BF16),
+            pltpu.VMEM((chips, brow, sb), BF16),
             pltpu.VMEM((2, chips, brow, pair), BF16),
             pltpu.VMEM((2, chips - 1, brow, pair), BF16),
+            dma,
+            dma,
             dma((5,)),
-            dma((SLOTS - 1,)),
-            dma((SLOTS - 1,)),
+            dma((2, SLOTS - 1)),
+            dma((2, SLOTS - 1)),
             dma((2, SLOTS - 1)),
             dma((2, SLOTS - 1)),
             dma((2,)),
@@ -390,7 +411,7 @@
                 out_shape=outs,
                 in_specs=[hbm] * len(outs),
                 out_specs=[hbm] * len(outs),
-                scratch_shapes=[dma((len(outs),))],
+                scratch_shapes=[pltpu.VMEM(o.shape, o.dtype) for o in outs] + [dma((len(outs),))] * 2,
                 compiler_params=pltpu.CompilerParams(vmem_limit_bytes=VMEM_LIMIT),
             )(*out)
         )

time: 56.7 us -> 30.9 us (0.54)
  Pallas kernels: 54 us -> 28.2 us
    pallas_call x1, Pallas kernels: 23 us -> 1.88 us  [shards(): pl.pallas_call(place, out_shape=outs, in_specs=[hbm] * len(outs), out_spe...]
    pallas_call x1, Pallas kernels: 31 us -> 26.3 us  [shards(): pl.pallas_call(functools.partial(kernel, n, direct), out_shape=outs, in_s...]
where the time goes in v3:
time: 30.9 us; the launch traced here: 30.7 us
  Pallas kernels  28.2 us (91%)
  between operations  2.58 us (8%)
    pallas_call x1, Pallas kernels, shards(): pl.pallas_call(functools.partial(kernel, n, direct), out_shape=outs, in_s...  26.3 us
    pallas_call x1, Pallas kernels, shards(): pl.pallas_call(place, out_shape=outs, in_specs=[hbm] * len(outs), out_spe...  1.88 us

profile of v3, /device:TPU:0, one launch (start us, length us, event | category | flops | bytes accessed | tf_op | source)
XLA Modules:
  0.0 30.7 jit_solution(8431419323101169034)
XLA Ops:
  2.6 26.3 %shard_map.119 = (bf16[256,512]{1,0:T(8,128)(2,1)}, bf16[256,512]{1,0:T(8,128)(2,1)}, bf16[128,512]{1,0:T(8,128)(2,1)}, f32[64,128]{1,0:T(8,128)}, f32[64,128]{1,0:T(8,128)}) custom-call(s32[1]{0:T(128)S(6)} %copy.13.refs_0_, s32[1]{0:T(128)S(6)} %copy.14.refs_1_, s32[1]{0:T(128)S(6)} %copy.15.refs_2_, bf16[256,512]{1,0:T(8,128)(2,1)} %refs_3_.1, ...), custom_call_target="tpu_custom_call" | custom-call | flops 2000000000 | bytes 4000000 | tf_op jit(solution)/shard_map/pallas_call | solution.py:355
  28.9 1.9 %shard_map.120 = (bf16[256,512]{1,0:T(8,128)(2,1)}, bf16[256,512]{1,0:T(8,128)(2,1)}, bf16[128,512]{1,0:T(8,128)(2,1)}, f32[64,128]{1,0:T(8,128)}, f32[64,128]{1,0:T(8,128)}) custom-call(bf16[256,512]{1,0:T(8,128)(2,1)} %get-tuple-element.10.refs_0_, bf16[256,512]{1,0:T(8,128)(2,1)} %get-tuple-element.11.refs_1_, ...), custom_call_target="tpu_custom_call" | custom-call | tf_op jit(solution)/shard_map/pallas_call | solution.py:409
